TPU v7x, 128 devices: a whole 4x4x4 slice. The times are simulated.
128 devices in a mesh: row: 16 (over x, y), col: 8 (over z, core).
Axes of the slice: x: 4, y: 4, z: 4, core: 2. Of those that a mesh axis runs over, the one named last changes fastest.
Arguments:
- panel: bfloat16 [49152, 256], P('row', 'col'), as said below
- trailing: bfloat16 [49152, 16384], P('row', 'col'), may hold values from -6 to 6
- tile_list: int32 [352], P('row'), may hold values from 0 to 23, as said below
Outputs:
- triangle: float32 [256, 256], replicated
- top_rows: float32 [16384, 256], P('col')
- updated: bfloat16 [45056, 16384], P('row', 'col')
Inputs may be any that keep to these rules, and one draw needn't show every extreme that they name: `tile_list`: each aligned block of 22 entries (the entries of one index of row) lists distinct tile numbers of that group's 24 tiles in increasing order and always includes tile 24 - 1. `panel`: the active rows of every row group, and all active rows together, have full column rank with a condition number under 100.
All inputs are finite; a program needn't handle non-finite values.
Results may differ from a plain program's by a relative error of at most 0.0065.
Values may be sent and summed in bfloat16 or wider, within the bound.
A program may use at most 128 MiB of HBM per device.

v0:
```python
import jax
import jax.numpy as jnp
from jax import lax
from jax.sharding import PartitionSpec as P

TILE = 128


def sent_to_all(array, axis):
    copies = jnp.broadcast_to(array, (lax.axis_size(axis), *array.shape))
    return lax.all_to_all(copies, axis, split_axis=0, concat_axis=0, tiled=True)


def laid_out(pieces, dim):
    pieces = jnp.moveaxis(pieces, 0, dim)
    shape = pieces.shape
    return pieces.reshape(*shape[:dim], shape[dim] * shape[dim + 1], *shape[dim + 2 :])


def gather_directly(array, axis, dim):
    pieces = sent_to_all(array, axis)
    return laid_out(pieces, dim)


def taken_together(array, axis):
    everything = sent_to_all(array, axis)
    return jnp.sum(everything.astype(jnp.float32), axis=0)


def pick_tiles(whole, tile_list):
    tiled = whole.reshape(-1, TILE, whole.shape[1])
    return jnp.take(tiled, tile_list, axis=0).reshape(-1, whole.shape[1])


def local(panel, trailing, tile_list):
    panel_full = gather_directly(panel, "col", 1)
    act_panel = pick_tiles(panel_full, tile_list)
    act_trail = pick_tiles(trailing, tile_list)
    local_gram = lax.dot_general(
        act_panel, act_panel, (((0,), (0,)), ((), ())), preferred_element_type=jnp.float32
    )
    gram_matrix = taken_together(local_gram.astype(jnp.bfloat16), "row").astype(jnp.float32)
    lower_factor = jnp.linalg.cholesky(gram_matrix)
    triangle = lower_factor.T
    local_cross = lax.dot_general(
        act_trail, act_panel, (((0,), (0,)), ((), ())), preferred_element_type=jnp.float32
    )
    cross_sum = lax.psum(local_cross, "row")
    top_rows = jax.scipy.linalg.solve_triangular(lower_factor, cross_sum.T, lower=True).T
    coeff = jax.scipy.linalg.solve_triangular(
        lower_factor, top_rows.T, lower=True, trans=1
    ).T.astype(jnp.bfloat16)
    product = lax.dot_general(
        act_panel, coeff, (((1,), (1,)), ((), ())), preferred_element_type=jnp.float32
    )
    updated = (act_trail.astype(jnp.float32) - product).astype(jnp.bfloat16)
    return (triangle, top_rows, updated)


def solution(mesh):
    return jax.shard_map(
        local,
        mesh=mesh,
        in_specs=(P("row", "col"), P("row", "col"), P("row")),
        out_specs=(P(), P("col", None), P("row", "col")),
        check_vma=False,
    )
```

profile of v0, /device:TPU:0, one launch (start us, length us, event | category | flops | bytes accessed | tf_op | source)
XLA Modules:
  0.0 185.2 jit_solution(9979115760256562924)
XLA Ops:
  7.2 2.3 %broadcast_in_dim.43 = bf16[8,3072,32]{1,2,0:T(8,128)(2,1)} broadcast(bf16[3072,32]{0,1:T(8,128)(2,1)} %param.3), dimensions={1,2} | broadcast | bytes 1769472 | tf_op jit(solution)/shard_map/broadcast_in_dim | solution.py:10
  9.4 5.4 %all-to-all-start = ((bf16[8,3072,32]{1,2,0:T(8,128)(2,1)}), bf16[8,3072,32]{1,2,0:T(8,128)(2,1)S(1)}, u32[]{:S(2)}, u32[]{:S(2)}) async-start(bf16[8,3072,32]{1,2,0:T(8,128)(2,1)} %broadcast_in_dim.43), calls=%async_computation | async-start | bytes 3145728 | tf_op jit(solution)/shard_map/all_to_all | solution.py:11
  14.9 21.5 %all-to-all-done = bf16[8,3072,32]{1,2,0:T(8,128)(2,1)S(1)} async-done(((bf16[8,3072,32]{1,2,0:T(8,128)(2,1)}), bf16[8,3072,32]{1,2,0:T(8,128)(2,1)S(1)}, u32[]{:S(2)}, u32[]{:S(2)}) %all-to-all-start) | async-done | bytes 1572896 | tf_op jit(solution)/shard_map/all_to_all | solution.py:11
  36.7 1.1 copy.17
  37.9 0.6 gather_fusion
  38.5 0.9 fusion.7
  39.4 1.5 broadcast_in_dim.46
  40.9 7.0 %all-to-all-start.1 = ((bf16[16,256,256]{2,1,0:T(8,128)(2,1)}), bf16[16,256,256]{2,1,0:T(8,128)(2,1)S(1)}, u32[]{:S(2)}, u32[]{:S(2)}) async-start(bf16[16,256,256]{2,1,0:T(8,128)(2,1)} %broadcast_in_dim.46), calls=%async_computation.1 | async-start | bytes 4194304 | tf_op jit(solution)/shard_map/all_to_all | solution.py:11
  48.0 10.5 %gather_fusion.1 = bf16[22,128,2048]{2,1,0:T(8,128)(2,1)} fusion(bf16[24,128,2048]{2,1,0:T(8,128)(2,1)} %bitcast.64, s32[1024]{0:T(1024)S(1)} %pad_clamp_fusion), kind=kCustom, calls=%fused_computation.1 | custom fusion | bytes 23068760 | tf_op jit(solution)/shard_map/jit(_take)/gather | solution.py:32
  58.5 8.8 %fusion.4 = f32[256,2048]{1,0:T(8,128)} fusion(bf16[22,128,2048]{2,1,0:T(8,128)(2,1)} %gather_fusion.1, pred[22]{0:T(512)(128)(4,1)S(1)} %compare_and_fusion, bf16[22,128,256]{2,1,0:T(8,128)(2,1)S(1)} %gather_fusion), kind=kOutput, calls=%fused_computation.11 | convolution fusion | flops 2959278080 | bytes 15073302 | tf_op jit(solution)/shard_map/dot_general | solution.py:45
  67.4 2.3 %bitcast_select_fusion.1 = bf16[2816,256]{1,0:T(8,128)(2,1)} fusion(bf16[22,128,256]{2,1,0:T(8,128)(2,1)S(1)} %gather_fusion, pred[2816]{0:T(1024)(128)(4,1)S(1)} %broadcast_bitcast_fusion), kind=kLoop, calls=%fused_computation.16 | loop fusion | flops 720896 | bytes 2886400 | tf_op jit(solution)/shard_map/jit(_take)/select_n | solution.py:32
  69.7 8.2 %all-to-all-done.1 = bf16[16,256,256]{2,1,0:T(8,128)(2,1)S(1)} async-done(((bf16[16,256,256]{2,1,0:T(8,128)(2,1)}), bf16[16,256,256]{2,1,0:T(8,128)(2,1)S(1)}, u32[]{:S(2)}, u32[]{:S(2)}) %all-to-all-start.1) | async-done | bytes 2097184 | tf_op jit(solution)/shard_map/all_to_all | solution.py:11
  78.4 11.7 %cholesky.50 = f32[128,128]{1,0:T(8,128)S(1)} custom-call(f32[128,128]{1,0:T(8,128)S(1)} %cholesky.118), custom_call_target="Cholesky" | custom-call | tf_op jit(solution)/shard_map/jit(cholesky)/cholesky | solution.py:43
  90.2 9.8 %custom-call.18 = f32[1,128,128]{1,2,0:T(8,128)S(1)} custom-call(f32[1,128,128]{2,1,0:T(8,128)S(1)} %get-tuple-element.35), custom_call_target="InvertDiagBlocksLowerTriangular" | custom-call | tf_op jit(solution)/shard_map/jit(cholesky)/cholesky | solution.py:43
  100.5 11.7 %cholesky.105 = f32[128,128]{1,0:T(8,128)S(1)} custom-call(f32[128,128]{1,0:T(8,128)S(1)} %convolution_subtract_fusion.2), custom_call_target="Cholesky" | custom-call | tf_op jit(solution)/shard_map/jit(cholesky)/cholesky | solution.py:43
  112.3 0.6 compare_reduce_fusion
  114.3 0.8 copy.21
  115.2 5.2 %while.1 = (s32[]{:T(128)}, f32[256,256]{1,0:T(8,128)S(1)}, s32[2,2]{1,0:T(2,128)S(1)}, f32[2,128,128]{2,1,0:T(8,128)}, s32[]{:T(128)}) while((s32[]{:T(128)}, f32[256,256]{1,0:T(8,128)S(1)}, s32[2,2]{1,0:T(2,128)S(1)}, f32[2,128,128]{2,1,0:T(8,128)}, s32[]{:T(128)}) %tuple.32), condition=%wide.while_cond, body=%wide.while_body.sunk | while | flops 2 | bytes 132205 | solution.py:49
  115.2 0.6 fusion.37
  115.8 2.0 %bitcast_dynamic-update-slice_fusion.2 = f32[2,128,128]{2,1,0:T(8,128)} fusion(f32[2,128,128]{2,1,0:T(8,128)} %get-tuple-element.79, s32[]{:T(128)S(6)} %copy.32, f32[256,256]{1,0:T(8,128)S(1)} %get-tuple-element.82, s32[]{:T(128)} %bitcast.62, s32[]{:T(128)} %bitcast.63), kind=kLoop, calls=%fused_computation.2.clone.1 | loop fusion | bytes 132100 | tf_op jit(solution)/shard_map/jit(_solve_triangular)/triangular_solve
  117.8 0.6 fusion.37
  118.3 2.0 %bitcast_dynamic-update-slice_fusion.2 = f32[2,128,128]{2,1,0:T(8,128)} fusion(f32[2,128,128]{2,1,0:T(8,128)} %get-tuple-element.79, s32[]{:T(128)S(6)} %copy.32, f32[256,256]{1,0:T(8,128)S(1)} %get-tuple-element.82, s32[]{:T(128)} %bitcast.62, s32[]{:T(128)} %bitcast.63), kind=kLoop, calls=%fused_computation.2.clone.1 | loop fusion | bytes 132100 | tf_op jit(solution)/shard_map/jit(_solve_triangular)/triangular_solve
  120.4 20.5 %custom-call.19 = f32[2,128,128]{1,2,0:T(8,128)S(1)} custom-call(f32[2,128,128]{2,1,0:T(8,128)} %get-tuple-element.10), custom_call_target="InvertDiagBlocksLowerTriangular" | custom-call | tf_op jit(solution)/shard_map/jit(_solve_triangular)/triangular_solve | solution.py:49
  140.9 16.8 %all-reduce.3.cloned.1.call-done = f32[256,2048]{1,0:T(8,128)} async-done(((f32[256,2048]{1,0:T(8,128)}), f32[256,2048]{1,0:T(8,128)}) %all-reduce.3.cloned.1.call-update) | async-done | bytes 2097168 | tf_op jit(solution)/shard_map/psum | solution.py:48
  157.7 2.4 %fusion.8 = f32[128,2048]{1,0:T(8,128)S(1)} fusion(f32[256,2048]{1,0:T(8,128)} %all-reduce.3.cloned.1.call-done, f32[2,128,128]{1,2,0:T(8,128)S(1)} %custom-call.19), kind=kOutput, calls=%fused_computation.21 | convolution fusion | flops 402653184 | bytes 2162688 | tf_op jit(solution)/shard_map/jit(_solve_triangular)/triangular_solve | solution.py:49
  160.1 1.0 convolution_subtract_fusion.1
  161.1 1.0 fusion.20
  162.2 1.8 fusion.27
  164.1 1.1 convolution_subtract_fusion
  165.2 1.8 convolution_convert_fusion
  167.0 1.8 copy.22
  168.9 9.5 %subtract_convert_fusion = bf16[2816,2048]{1,0:T(8,128)(2,1)} fusion(bf16[22,128,2048]{2,1,0:T(8,128)(2,1)} %gather_fusion.1, pred[2816]{0:T(1024)(128)(4,1)S(1)} %broadcast_bitcast_fusion, bf16[2816,256]{1,0:T(8,128)(2,1)S(1)} %copy-done.1, bf16[128,2048]{1,0:T(8,128)(2,1)} %get-tuple-element.38, bf16[128,2048]{1,0:T(8,128)(2,1)} %convolution_convert_fusion), kind=kOutput, calls=%fused_computation.4 | convolution fusion | flops 2977955840 | bytes 25561856 | tf_op jit(solution)/shard_map/dot_general | solution.py:53
  (29 shorter events, 1.7 us)
Async XLA Ops:
  7.2 7.7 %copy-start.2 = (s32[22]{0:T(128)S(1)}, s32[22]{0:T(128)}, u32[]{:S(2)}) copy-start(s32[22]{0:T(128)} %param.5) | copy-start | bytes 268
  9.4 27.0 %all-to-all-start = ((bf16[8,3072,32]{1,2,0:T(8,128)(2,1)}), bf16[8,3072,32]{1,2,0:T(8,128)(2,1)S(1)}, u32[]{:S(2)}, u32[]{:S(2)}) async-start(bf16[8,3072,32]{1,2,0:T(8,128)(2,1)} %broadcast_in_dim.43), calls=%async_computation | async-start | bytes 3145728 | tf_op jit(solution)/shard_map/all_to_all | solution.py:11
  40.9 37.0 %all-to-all-start.1 = ((bf16[16,256,256]{2,1,0:T(8,128)(2,1)}), bf16[16,256,256]{2,1,0:T(8,128)(2,1)S(1)}, u32[]{:S(2)}, u32[]{:S(2)}) async-start(bf16[16,256,256]{2,1,0:T(8,128)(2,1)} %broadcast_in_dim.46), calls=%async_computation.1 | async-start | bytes 4194304 | tf_op jit(solution)/shard_map/all_to_all | solution.py:11
  48.0 109.7 %all-reduce.3.cloned.1.call-start = ((), (), s32[]{:S(2)}) async-start(), calls=%async_computation.2 | async-start | bytes 4194304 | tf_op jit(solution)/shard_map/psum | solution.py:48
  157.7 2.4 %copy-start = (f32[256,2048]{1,0:T(8,128)S(1)}, f32[256,2048]{1,0:T(8,128)}, u32[]{:S(2)}) copy-start(f32[256,2048]{1,0:T(8,128)} %all-reduce.3.cloned.1.call-done) | copy-start | bytes 6291460
  167.0 1.8 copy-start.1
Sparse Core Ops, SparseCore 0:
  67.5 90.1 all-reduce.2
where the time goes:
time: 186 us; the launch traced here: 185 us
  other arithmetic  57.3 us (31%)
  waiting for transfers between devices  46.5 us (25%)
  matrix products  28.8 us (15%)
  local copies, waits for them, and re-layouts  24.5 us (13%)
  between operations  15.5 us (8%)
  starting transfers between devices  12.5 us (7%)
    another operation x6, other arithmetic, local(): lower_factor = jnp.linalg.cholesky(gram_matrix)  34 us
    all_to_all x2, waiting for transfers between devices, sent_to_all(): return lax.all_to_all(copies, axis, split_axis=0, concat_axis=0, tiled=True)  29.7 us
    another operation x3, other arithmetic, local(): jax.scipy.linalg.solve_triangular(lower_factor, cross_sum.T, lower=True)  20.5 us
    psum x1, waiting for transfers between devices, local(): cross_sum = lax.psum(local_cross, 'row')  16.8 us
    all_to_all x2, starting transfers between devices, sent_to_all(): return lax.all_to_all(copies, axis, split_axis=0, concat_axis=0, tiled=True)  12.4 us
    gather x2, local copies, waits for them, and re-layouts, pick_tiles(): return jnp.take(tiled, tile_list, axis=0).reshape(-1, whole.shape[1])  11.1 us
    dot_general x1, matrix products, local(): lax.dot_general(act_panel, coeff, (((1,), (1,)), ((), ())), preferred_ele...  9.49 us
    dot_general x1, matrix products, local(): lax.dot_general(act_trail, act_panel, (((0,), (0,)), ((), ())), preferred...  8.84 us
  transfers between devices with their start and end apart: 3, of which 3 were waited for; matrix products, arithmetic and copies ran while one was open for 45% of the time, Pallas kernels for 0%

commit v1 on v0

--- a/solution.py
+++ b/solution.py
@@ -45,7 +45,7 @@
     local_cross = lax.dot_general(
         act_trail, act_panel, (((0,), (0,)), ((), ())), preferred_element_type=jnp.float32
     )
-    cross_sum = lax.psum(local_cross, "row")
+    cross_sum = jnp.sum(lax.all_gather(local_cross, "row"), axis=0)
     top_rows = jax.scipy.linalg.solve_triangular(lower_factor, cross_sum.T, lower=True).T
     coeff = jax.scipy.linalg.solve_triangular(
         lower_factor, top_rows.T, lower=True, trans=1

time: 186 us -> 305 us (1.64)
  waiting for transfers between devices: 46.5 us -> 150 us
  other arithmetic: 57.3 us -> 69.4 us
    all_gather x0 -> x1, waiting for transfers between devices: none -> 97 us  [local(): cross_sum = jnp.sum(lax.all_gather(local_cross, 'row'), axis=0)]
    all_to_all x2, waiting for transfers between devices: 29.7 us -> 53.2 us  [sent_to_all(): return lax.all_to_all(copies, axis, split_axis=0, concat_axis=0, tiled=True)]
    psum x1 -> x0, waiting for transfers between devices: 16.8 us -> none  [local(): cross_sum = lax.psum(local_cross, 'row')]
    reduce_sum x0 -> x1, other arithmetic: none -> 12.1 us  [local(): cross_sum = jnp.sum(lax.all_gather(local_cross, 'row'), axis=0)]
  transfers between devices with their start and end apart: 3 -> 3, of which waited for: 3 -> 3; matrix products, arithmetic and copies ran while one was open for 45% -> 25% of each run, Pallas kernels for 0% -> 0%
where the time goes in v1:
time: 305 us; the launch traced here: 304 us
  waiting for transfers between devices  150 us (49%)
  other arithmetic  69.4 us (23%)
  matrix products  30.1 us (10%)
  local copies, waits for them, and re-layouts  26.3 us (9%)
  between operations  15.6 us (5%)
  starting transfers between devices  12.5 us (4%)
    all_gather x1, waiting for transfers between devices, local(): cross_sum = jnp.sum(lax.all_gather(local_cross, 'row'), axis=0)  97 us
    all_to_all x2, waiting for transfers between devices, sent_to_all(): return lax.all_to_all(copies, axis, split_axis=0, concat_axis=0, tiled=True)  53.2 us
    another operation x6, other arithmetic, local(): lower_factor = jnp.linalg.cholesky(gram_matrix)  33.9 us
    another operation x3, other arithmetic, local(): jax.scipy.linalg.solve_triangular(lower_factor, cross_sum.T, lower=True)  20.5 us
    all_to_all x2, starting transfers between devices, sent_to_all(): return lax.all_to_all(copies, axis, split_axis=0, concat_axis=0, tiled=True)  12.4 us
    reduce_sum x1, other arithmetic, local(): cross_sum = jnp.sum(lax.all_gather(local_cross, 'row'), axis=0)  12.1 us
    gather x2, local copies, waits for them, and re-layouts, pick_tiles(): return jnp.take(tiled, tile_list, axis=0).reshape(-1, whole.shape[1])  11 us
    dot_general x1, matrix products, local(): lax.dot_general(act_trail, act_panel, (((0,), (0,)), ((), ())), preferred...  9.38 us
  transfers between devices with their start and end apart: 3, of which 3 were waited for; matrix products, arithmetic and copies ran while one was open for 25% of the time, Pallas kernels for 0%

profile of v1, /device:TPU:0, one launch (start us, length us, event | category | flops | bytes accessed | tf_op | source)
XLA Modules:
  0.0 304.0 jit_solution(12988428908643971038)
XLA Ops:
  7.2 2.3 broadcast_in_dim.43
  9.4 5.4 %all-to-all-start = ((bf16[8,3072,32]{1,2,0:T(8,128)(2,1)}), bf16[8,3072,32]{1,2,0:T(8,128)(2,1)S(1)}, u32[]{:S(2)}, u32[]{:S(2)}) async-start(bf16[8,3072,32]{1,2,0:T(8,128)(2,1)} %broadcast_in_dim.43), calls=%async_computation | async-start | bytes 3145728 | tf_op jit(solution)/shard_map/all_to_all | solution.py:11
  14.9 10.4 %gather_fusion.1 = bf16[22,128,2048]{2,1,0:T(8,128)(2,1)} fusion(bf16[24,128,2048]{2,1,0:T(8,128)(2,1)} %bitcast.67, s32[1024]{0:T(1024)S(1)} %pad_clamp_fusion), kind=kCustom, calls=%fused_computation.1 | custom fusion | bytes 23068760 | tf_op jit(solution)/shard_map/jit(_take)/gather | solution.py:32
  25.3 11.1 %all-to-all-done = bf16[8,3072,32]{1,2,0:T(8,128)(2,1)S(1)} async-done(((bf16[8,3072,32]{1,2,0:T(8,128)(2,1)}), bf16[8,3072,32]{1,2,0:T(8,128)(2,1)S(1)}, u32[]{:S(2)}, u32[]{:S(2)}) %all-to-all-start) | async-done | bytes 1572896 | tf_op jit(solution)/shard_map/all_to_all | solution.py:11
  36.7 1.1 copy.32
  37.9 0.6 gather_fusion
  38.5 9.4 %fusion.4 = f32[2048,256]{1,0:T(8,128)} fusion(bf16[22,128,2048]{2,1,0:T(8,128)(2,1)} %gather_fusion.1, pred[22]{0:T(512)(128)(4,1)S(1)} %compare_and_fusion, bf16[22,128,256]{2,1,0:T(8,128)(2,1)S(1)} %gather_fusion), kind=kOutput, calls=%fused_computation.11 | convolution fusion | flops 2959278080 | bytes 15073302 | tf_op jit(solution)/shard_map/dot_general | solution.py:45
  47.9 0.9 fusion.7
  48.8 1.5 broadcast_in_dim.46
  50.3 7.0 %all-to-all-start.1 = ((bf16[16,256,256]{2,1,0:T(8,128)(2,1)}), bf16[16,256,256]{2,1,0:T(8,128)(2,1)S(1)}, u32[]{:S(2)}, u32[]{:S(2)}) async-start(bf16[16,256,256]{2,1,0:T(8,128)(2,1)} %broadcast_in_dim.46), calls=%async_computation.1 | async-start | bytes 4194304 | tf_op jit(solution)/shard_map/all_to_all | solution.py:11
  57.5 2.3 bitcast_select_fusion.1
  59.8 42.1 %all-to-all-done.1 = bf16[16,256,256]{2,1,0:T(8,128)(2,1)S(1)} async-done(((bf16[16,256,256]{2,1,0:T(8,128)(2,1)}), bf16[16,256,256]{2,1,0:T(8,128)(2,1)S(1)}, u32[]{:S(2)}, u32[]{:S(2)}) %all-to-all-start.1) | async-done | bytes 2097184 | tf_op jit(solution)/shard_map/all_to_all | solution.py:11
  102.4 11.7 %cholesky.50 = f32[128,128]{1,0:T(8,128)S(1)} custom-call(f32[128,128]{1,0:T(8,128)S(1)} %cholesky.118), custom_call_target="Cholesky" | custom-call | tf_op jit(solution)/shard_map/jit(cholesky)/cholesky | solution.py:43
  114.1 9.8 %custom-call.18 = f32[1,128,128]{1,2,0:T(8,128)S(1)} custom-call(f32[1,128,128]{2,1,0:T(8,128)S(1)} %get-tuple-element.41), custom_call_target="InvertDiagBlocksLowerTriangular" | custom-call | tf_op jit(solution)/shard_map/jit(cholesky)/cholesky | solution.py:43
  124.4 11.7 %cholesky.105 = f32[128,128]{1,0:T(8,128)S(1)} custom-call(f32[128,128]{1,0:T(8,128)S(1)} %convolution_subtract_fusion.2), custom_call_target="Cholesky" | custom-call | tf_op jit(solution)/shard_map/jit(cholesky)/cholesky | solution.py:43
  136.2 0.6 compare_reduce_fusion
  138.2 0.8 copy.37
  139.1 5.3 %while.1 = (s32[]{:T(128)}, f32[256,256]{1,0:T(8,128)S(1)}, s32[2,2]{1,0:T(2,128)S(1)}, f32[2,128,128]{2,1,0:T(8,128)}, s32[]{:T(128)}) while((s32[]{:T(128)}, f32[256,256]{1,0:T(8,128)S(1)}, s32[2,2]{1,0:T(2,128)S(1)}, f32[2,128,128]{2,1,0:T(8,128)}, s32[]{:T(128)}) %tuple.34), condition=%wide.while_cond, body=%wide.while_body.sunk | while | flops 2 | bytes 132205 | solution.py:49
  139.7 2.0 bitcast_dynamic-update-slice_fusion.2
  142.3 2.0 bitcast_dynamic-update-slice_fusion.2
  144.4 20.5 %custom-call.19 = f32[2,128,128]{1,2,0:T(8,128)S(1)} custom-call(f32[2,128,128]{2,1,0:T(8,128)} %get-tuple-element.10), custom_call_target="InvertDiagBlocksLowerTriangular" | custom-call | tf_op jit(solution)/shard_map/jit(_solve_triangular)/triangular_solve | solution.py:49
  164.9 97.0 %all-gather.3.cloned.1.call-done = f32[32768,256]{1,0:T(8,128)} async-done(((f32[2048,256]{1,0:T(8,128)}), f32[32768,256]{1,0:T(8,128)}) %all-gather.3.cloned.1.call-update) | async-done | bytes 33554448 | tf_op jit(solution)/shard_map/all_gather | solution.py:48
  261.9 12.1 %reduce_sum.19 = f32[2048,256]{1,0:T(8,128)S(1)} reduce(f32[16,2048,256]{2,1,0:T(8,128)} %bitcast.66, f32[]{:T(128)} %constant.112.clone.1), dimensions={0}, to_apply=%region_5.6 | reduce | flops 7864320 | bytes 35651588 | tf_op jit(solution)/shard_map/reduce_sum | solution.py:48
  273.9 1.8 copy.36
  275.7 2.4 fusion.8
  278.2 1.0 convolution_subtract_fusion.1
  279.2 1.1 fusion.20
  280.4 2.1 fusion.27
  282.6 1.8 copy.38
  284.4 2.4 convolution_subtract_fusion
  286.8 1.0 convolution_convert_fusion
  287.8 9.3 %subtract_convert_fusion = bf16[2816,2048]{1,0:T(8,128)(2,1)} fusion(bf16[22,128,2048]{2,1,0:T(8,128)(2,1)} %gather_fusion.1, pred[2816]{0:T(1024)(128)(4,1)S(1)} %broadcast_bitcast_fusion, bf16[2816,256]{1,0:T(8,128)(2,1)S(1)} %copy-done.1, bf16[128,2048]{1,0:T(8,128)(2,1)S(1)} %copy-done.2, bf16[128,2048]{1,0:T(8,128)(2,1)S(1)} %convolution_convert_fusion), kind=kOutput, calls=%fused_computation.4 | convolution fusion | flops 2977955840 | bytes 25561856 | tf_op jit(solution)/shard_map/dot_general | solution.py:53
  (33 shorter events, 3.0 us)
Async XLA Ops:
  7.2 7.7 %copy-start.3 = (s32[22]{0:T(128)S(1)}, s32[22]{0:T(128)}, u32[]{:S(2)}) copy-start(s32[22]{0:T(128)} %param.5) | copy-start | bytes 268
  9.4 27.0 %all-to-all-start = ((bf16[8,3072,32]{1,2,0:T(8,128)(2,1)}), bf16[8,3072,32]{1,2,0:T(8,128)(2,1)S(1)}, u32[]{:S(2)}, u32[]{:S(2)}) async-start(bf16[8,3072,32]{1,2,0:T(8,128)(2,1)} %broadcast_in_dim.43), calls=%async_computation | async-start | bytes 3145728 | tf_op jit(solution)/shard_map/all_to_all | solution.py:11
  14.8 247.0 %all-gather.3.cloned.1.call-start = ((), (), s32[]{:S(2)}) async-start(), calls=%async_computation.2 | async-start | bytes 35651584 | tf_op jit(solution)/shard_map/all_gather | solution.py:48
  50.3 51.5 %all-to-all-start.1 = ((bf16[16,256,256]{2,1,0:T(8,128)(2,1)}), bf16[16,256,256]{2,1,0:T(8,128)(2,1)S(1)}, u32[]{:S(2)}, u32[]{:S(2)}) async-start(bf16[16,256,256]{2,1,0:T(8,128)(2,1)} %broadcast_in_dim.46), calls=%async_computation.1 | async-start | bytes 4194304 | tf_op jit(solution)/shard_map/all_to_all | solution.py:11
  275.7 2.4 copy-start
  284.4 3.4 %copy-start.1 = (bf16[2816,256]{1,0:T(8,128)(2,1)S(1)}, bf16[2816,256]{1,0:T(8,128)(2,1)}, u32[]{:S(2)}) copy-start(bf16[2816,256]{1,0:T(8,128)(2,1)} %bitcast_select_fusion.1) | copy-start | bytes 4325380
  284.4 3.4 %copy-start.2 = (bf16[128,2048]{1,0:T(8,128)(2,1)S(1)}, bf16[128,2048]{1,0:T(8,128)(2,1)}, u32[]{:S(2)}) copy-start(bf16[128,2048]{1,0:T(8,128)(2,1)} %get-tuple-element.44) | copy-start | bytes 1572868
Sparse Core Ops, SparseCore 0:
  48.0 213.7 all-gather.2
